TPU v7x, 512 devices: a whole 4x8x8 slice. The times are simulated.
512 devices in a mesh: dp: 16 (over z, core), ctx: 32 (over x, y).
Axes of the slice: x: 4, y: 8, z: 8, core: 2. Of those that a mesh axis runs over, the one named last changes fastest.
Arguments:
- frames: bfloat16 [512, 2, 512, 512], P(('dp', 'ctx')), parts along dimension 0, may hold values from -6 to 6
- episode_lengths: int32 [1024], P('dp'), parts along dimension 0, may hold values from 1 to 1024, 32768 in all
- w_qkv: bfloat16 [512, 1536], replicated, may hold values from -1 to 1
- w_out: bfloat16 [512, 512], replicated, may hold values from -0.25 to 0.25
Outputs:
- attended: bfloat16 [512, 2, 512, 512], P(('dp', 'ctx')), parts along dimension 0
There are 16 independent parts, one for each index of `dp`. A program takes and returns all parts, laid end to end along the dimension named above; an argument that names none is the same for every part. Nothing has to cross between parts.
Inputs may be any that keep to these rules, and one draw needn't show every extreme that they name: `episode_lengths`: the lengths sum to 32768; the longest is exactly 1024 tokens.
All inputs are finite; a program needn't handle non-finite values.
Results may differ from a plain program's by a relative error of at most 0.0082.
Values may be sent and summed in bfloat16 or wider, within the bound.
A program may use at most 64 MiB of HBM per device.

v0:
```python
import jax
import jax.numpy as jnp
from jax import lax
from jax.sharding import PartitionSpec as P

HEADS = 4
HEAD_DIM = 128
WIN = 2


def from_behind(block, axis, distance):
    devices = range(lax.axis_size(axis))
    route = [(i - distance, i) for i in devices if i - distance in devices]
    return lax.ppermute(block, axis, route)


def normalize(rows):
    wide = rows.astype(jnp.float32)
    factor = lax.rsqrt(jnp.mean(wide * wide, axis=-1, keepdims=True) + 1e-06)
    return (wide * factor).astype(jnp.bfloat16)


def episode_start(positions, episode_lengths):
    ends = jnp.cumsum(episode_lengths)
    passed = (ends[None, :] <= positions[:, None]).astype(jnp.int32)
    return jnp.sum(passed * episode_lengths[None, :], axis=1)


def head_scores(query_part, key_part):
    scores = lax.dot_general(
        query_part, key_part, (((1,), (1,)), ((), ())), preferred_element_type=jnp.float32
    )
    return scores * HEAD_DIM ** (-0.5)


def attend(queries, keys, values, allowed):
    outputs = []
    for head in range(HEADS):
        low = head * HEAD_DIM
        high = low + HEAD_DIM
        query_part = queries[:, low:high]
        scores = head_scores(query_part, keys[:, low:high])
        scores = jnp.where(allowed, scores, -jnp.inf)
        peak = jnp.max(scores, axis=1, keepdims=True)
        weights = jnp.exp(scores - peak)
        totals = jnp.sum(weights, axis=1, keepdims=True)
        mixed = (
            jnp.dot(
                weights.astype(jnp.bfloat16),
                values[:, low:high],
                preferred_element_type=jnp.float32,
            )
            / totals
        )
        outputs.append(mixed)
    return jnp.concatenate(outputs, axis=1).astype(jnp.bfloat16)


def local(frames, episode_lengths, w_qkv, w_out):
    width = w_out.shape[0]
    group = frames.shape[2]
    count = lax.axis_size("ctx")
    place = lax.axis_index("ctx")
    normed = normalize(frames[0])
    projected = (
        jnp.dot(normed.reshape(2 * group, width), w_qkv, preferred_element_type=jnp.float32)
        .astype(jnp.bfloat16)
        .reshape(2, group, 3 * width)
    )
    carried = projected[:, :, width:]
    low_now = carried[0]
    high_now = carried[1]
    low_window = []
    high_window = []
    for step in range(WIN):
        low_next = from_behind(low_now, "ctx", 1)
        high_arrived = from_behind(high_now, "ctx", -1)
        high_next = jnp.where(place == count - 1, low_now, high_arrived)
        low_window.append(low_next)
        high_window.append(high_next)
        low_now = low_next
        high_now = high_next
    received = jnp.stack(low_window[::-1] + high_window[::-1], axis=0)
    results = []
    for half in range(2):
        block_index = place if half == 0 else 2 * count - 1 - place
        earlier = received[half * WIN : (half + 1) * WIN].reshape(WIN * group, 2 * width)
        pairs = jnp.concatenate([earlier, projected[half, :, width:]], axis=0)
        first = block_index * group
        query_pos = first + jnp.arange(group, dtype=jnp.int32)
        key_pos = first - WIN * group + jnp.arange((WIN + 1) * group, dtype=jnp.int32)
        starts = episode_start(query_pos, episode_lengths)
        allowed = (key_pos[None, :] <= query_pos[:, None]) & (key_pos[None, :] >= starts[:, None])
        mixed = attend(projected[half, :, :width], pairs[:, :width], pairs[:, width:], allowed)
        results.append(
            jnp.dot(mixed, w_out, preferred_element_type=jnp.float32).astype(jnp.bfloat16)
        )
    return jnp.stack(results, axis=0)[None]


def solution(mesh):
    in_specs = (P(("dp", "ctx"), None, None, None), P("dp"), P(), P())
    out_specs = P(("dp", "ctx"), None, None, None)
    return jax.shard_map(local, mesh=mesh, in_specs=in_specs, out_specs=out_specs, check_vma=False)
```

profile of v0, /device:TPU:56, one launch (start us, length us, event | category | flops | bytes accessed | tf_op | source)
XLA Modules:
  0.0 98.3 jit_solution(15566635817657565689)
XLA Ops:
  0.0 1.6 %multiply_reduce_fusion = f32[2,512]{1,0:T(2,128)S(1)} fusion(bf16[1,2,512,512]{3,2,1,0:T(8,128)(2,1)} %param.4), kind=kLoop, calls=%fused_computation.75 | loop fusion | flops 1571840 | bytes 1052672 | tf_op jit(solution)/shard_map/reduce_sum | solution.py:19
  1.7 1.5 %fusion.24 = bf16[1024,512]{1,0:T(8,128)(2,1)S(1)} fusion(f32[1024]{0:T(1024)S(1)} %bitcast.56, bf16[1,2,512,512]{3,2,1,0:T(8,128)(2,1)} %param.4), kind=kLoop, calls=%fused_computation.74 | loop fusion | flops 1572864 | bytes 2101248 | tf_op jit(solution)/shard_map/convert_element_type | solution.py:20
  3.2 1.8 %convolution_convert_fusion = bf16[1024,1536]{1,0:T(8,128)(2,1)S(1)} fusion(bf16[1024,512]{1,0:T(8,128)(2,1)S(1)} %fusion.24, bf16[512,1536]{1,0:T(8,128)(2,1)S(1)} %copy-done), kind=kOutput, calls=%fused_computation.28 | convolution fusion | flops 1612185600 | bytes 5767168 | tf_op jit(solution)/shard_map/dot_general | solution.py:66
  5.0 1.5 %slice_bitcast_fusion.1 = (bf16[512,1024]{1,0:T(8,128)(2,1)S(1)}, bf16[512,1024]{1,0:T(8,128)(2,1)}) fusion(bf16[2,512,1536]{2,1,0:T(8,128)(2,1)S(1)} %bitcast.52), kind=kLoop, calls=%fused_computation.113 | loop fusion | bytes 4194304 | tf_op jit(solution)/shard_map/squeeze | solution.py:71
  6.5 3.2 %collective-permute-start.2 = (bf16[512,1024]{1,0:T(8,128)(2,1)}, bf16[512,1024]{1,0:T(8,128)(2,1)}, u32[]{:S(2)}, u32[]{:S(2)}) collective-permute-start(bf16[512,1024]{1,0:T(8,128)(2,1)} %get-tuple-element.10), channel_id=1, source_target_pairs={{1,0},{2,1},{3,2},{4,3},{5,4},{6,5},{7,6},{8,7},{9,8},{10,9},{11,1... | collective-permute-start | bytes 3145736 | tf_op jit(solution)/shard_map/ppermute | solution.py:14
  9.7 4.7 %collective-permute-start = (bf16[512,1024]{1,0:T(8,128)(2,1)S(1)}, bf16[512,1024]{1,0:T(8,128)(2,1)}, u32[]{:S(2)}, u32[]{:S(2)}) collective-permute-start(bf16[512,1024]{1,0:T(8,128)(2,1)S(1)} %get-tuple-element.9), channel_id=1, source_target_pairs={{0,1},{1,2},{2,3},{3,4},{4,5},{5,6},{6,7},{7,8},{8,9},{9,10},{10,1... | collective-permute-start | bytes 3145736 | tf_op jit(solution)/shard_map/ppermute | solution.py:14
  14.4 21.2 %collective-permute-done.2 = bf16[512,1024]{1,0:T(8,128)(2,1)} collective-permute-done((bf16[512,1024]{1,0:T(8,128)(2,1)}, bf16[512,1024]{1,0:T(8,128)(2,1)}, u32[]{:S(2)}, u32[]{:S(2)}) %collective-permute-start.2) | collective-permute-done | bytes 1048608 | tf_op jit(solution)/shard_map/ppermute | solution.py:14
  35.7 2.6 %broadcast_select_fusion = bf16[512,1024]{1,0:T(8,128)(2,1)} fusion(bf16[512,1024]{1,0:T(8,128)(2,1)} %collective-permute-done.2, pred[]{:T(512)S(6)} %eq.4, bf16[2,512,1536]{2,1,0:T(8,128)(2,1)} %bitcast.53), kind=kLoop, calls=%fused_computation.116 | loop fusion | flops 524288 | bytes 3145729 | tf_op jit(solution)/shard_map/jit(_where)/select_n | solution.py:78
  38.3 1.9 %collective-permute-start.3 = (bf16[512,1024]{1,0:T(8,128)(2,1)}, bf16[512,1024]{1,0:T(8,128)(2,1)}, u32[]{:S(2)}, u32[]{:S(2)}) collective-permute-start(bf16[512,1024]{1,0:T(8,128)(2,1)} %broadcast_select_fusion), channel_id=1, source_target_pairs={{1,0},{2,1},{3,2},{4,3},{5,4},{6,5},{7,6},{8,7},{9,8},{10,9},{11,1... | collective-permute-start | bytes 3145736 | tf_op jit(solution)/shard_map/ppermute | solution.py:14
  40.7 1.3 %slice_bitcast_fusion.3 = (bf16[512,512]{1,0:T(8,128)(2,1)S(1)}, bf16[512,512]{1,0:T(8,128)(2,1)S(1)}) fusion(bf16[2,512,1536]{2,1,0:T(8,128)(2,1)} %bitcast.54), kind=kLoop, calls=%fused_computation.118 | loop fusion | bytes 2097152 | tf_op jit(solution)/shard_map/squeeze | solution.py:94
  42.0 6.2 %collective-permute-start.1 = (bf16[512,1024]{1,0:T(8,128)(2,1)}, bf16[512,1024]{1,0:T(8,128)(2,1)S(1)}, u32[]{:S(2)}, u32[]{:S(2)}) collective-permute-start(bf16[512,1024]{1,0:T(8,128)(2,1)} %collective-permute-done), channel_id=1, source_target_pairs={{0,1},{1,2},{2,3},{3,4},{4,5},{5,6},{6,7},{7,8},{8,9},{9,10},{10,1... | collective-permute-start | bytes 3145736 | tf_op jit(solution)/shard_map/ppermute | solution.py:14
  48.2 18.4 %collective-permute-done.3 = bf16[512,1024]{1,0:T(8,128)(2,1)} collective-permute-done((bf16[512,1024]{1,0:T(8,128)(2,1)}, bf16[512,1024]{1,0:T(8,128)(2,1)}, u32[]{:S(2)}, u32[]{:S(2)}) %collective-permute-start.3) | collective-permute-done | bytes 1048608 | tf_op jit(solution)/shard_map/ppermute | solution.py:14
  66.6 1.3 %select_bitcast_fusion = bf16[1,512,1024]{2,1,0:T(8,128)(2,1)S(1)} fusion(bf16[512,1024]{1,0:T(8,128)(2,1)} %collective-permute-done, bf16[512,1024]{1,0:T(8,128)(2,1)} %collective-permute-done.3, pred[]{:T(512)S(6)} %eq.4), kind=kLoop, calls=%fused_computation.115 | loop fusion | flops 524288 | bytes 3145729 | tf_op jit(solution)/shard_map/stack | solution.py:83
  68.0 1.4 %pad_maximum_fusion.1 = bf16[2,512,1024]{2,1,0:T(8,128)(2,1)S(1)} fusion(bf16[1,512,1024]{2,1,0:T(8,128)(2,1)} %bitcast.12, bf16[1,512,1024]{2,1,0:T(8,128)(2,1)S(1)} %select_bitcast_fusion), kind=kLoop, calls=%fused_computation.72 | loop fusion | flops 1048576 | bytes 4194304 | tf_op jit(solution)/shard_map/stack | solution.py:83
  69.4 1.8 %fusion.169 = (f32[512]{0:T(512)S(1)}, f32[512,1536]{1,0:T(8,128)S(1)}) fusion(bf16[1024,1024]{1,0:T(8,128)(2,1)S(1)} %bitcast.44, bf16[512,1024]{1,0:T(8,128)(2,1)} %get-tuple-element.10, bf16[512,512]{1,0:T(8,128)(2,1)S(1)} %get-tuple-element.8, s32[512]{0:T(512)S(1)} %get-tuple-element.6, s32[512]{0:T(512)S(1)} %iota_add_fusion.2, ...), kind=kOutput, calls=%fused_computation.184 | convolution fusion | flops 206831104 | bytes 6436864 | tf_op jit(solution)/shard_map/dot_general | solution.py:30
  71.2 1.8 %fusion.170 = (f32[512]{0:T(512)S(1)}, f32[512,1536]{1,0:T(8,128)S(1)}) fusion(bf16[1024,1024]{1,0:T(8,128)(2,1)S(1)} %bitcast.45, bf16[512,1024]{1,0:T(8,128)(2,1)} %get-tuple-element.10, bf16[512,512]{1,0:T(8,128)(2,1)S(1)} %get-tuple-element.8, s32[512]{0:T(512)S(1)} %get-tuple-element.6, s32[512]{0:T(512)S(1)} %iota_add_fusion.2, ...), kind=kOutput, calls=%fused_computation.185 | convolution fusion | flops 206831104 | bytes 6436864 | tf_op jit(solution)/shard_map/dot_general | solution.py:30
  73.0 1.8 %fusion.171 = (f32[512]{0:T(512)S(1)}, f32[512,1536]{1,0:T(8,128)S(1)}) fusion(bf16[1024,1024]{1,0:T(8,128)(2,1)S(1)} %bitcast.46, bf16[512,1024]{1,0:T(8,128)(2,1)} %get-tuple-element.10, bf16[512,512]{1,0:T(8,128)(2,1)S(1)} %get-tuple-element.8, s32[512]{0:T(512)S(1)} %get-tuple-element.6, s32[512]{0:T(512)S(1)} %iota_add_fusion.2, ...), kind=kOutput, calls=%fused_computation.186 | convolution fusion | flops 206831104 | bytes 6436864 | tf_op jit(solution)/shard_map/dot_general | solution.py:30
  74.8 1.8 %fusion.172 = (f32[512]{0:T(512)S(1)}, f32[512,1536]{1,0:T(8,128)S(1)}) fusion(bf16[1024,1024]{1,0:T(8,128)(2,1)S(1)} %bitcast.47, bf16[512,1024]{1,0:T(8,128)(2,1)} %get-tuple-element.10, bf16[512,512]{1,0:T(8,128)(2,1)S(1)} %get-tuple-element.8, s32[512]{0:T(512)S(1)} %get-tuple-element.6, s32[512]{0:T(512)S(1)} %iota_add_fusion.2, ...), kind=kOutput, calls=%fused_computation.187 | convolution fusion | flops 206831104 | bytes 6436864 | tf_op jit(solution)/shard_map/dot_general | solution.py:30
  76.6 1.4 %pad_maximum_fusion = bf16[2,512,1024]{2,1,0:T(8,128)(2,1)S(1)} fusion(bf16[1,512,1024]{2,1,0:T(8,128)(2,1)} %bitcast.6, bf16[1,512,1024]{2,1,0:T(8,128)(2,1)S(1)} %bitcast.55), kind=kLoop, calls=%fused_computation.71 | loop fusion | flops 1048576 | bytes 4194304 | tf_op jit(solution)/shard_map/stack | solution.py:83
  82.3 1.6 %fusion.75 = bf16[512,128]{0,1:T(8,128)(2,1)S(1)} fusion(f32[512,1536]{1,0:T(8,128)S(1)} %get-tuple-element.12, f32[512]{0:T(512)S(1)} %get-tuple-element.11, bf16[512,1024]{1,0:T(8,128)(2,1)} %get-tuple-element.10, bf16[1024,1024]{1,0:T(8,128)(2,1)S(1)} %bitcast.48, f32[512]{0:T(512)S(1)} %fusion.22), kind=kOutput, calls=%fused_computation.104 | convolution fusion | flops 203816960 | bytes 6426624 | tf_op jit(solution)/shard_map/dot_general | solution.py:48
  84.5 1.6 %fusion.78 = bf16[512,128]{0,1:T(8,128)(2,1)S(1)} fusion(f32[512,1536]{1,0:T(8,128)S(1)} %get-tuple-element.14, f32[512]{0:T(512)S(1)} %get-tuple-element.13, bf16[1024,1024]{1,0:T(8,128)(2,1)S(1)} %bitcast.49, bf16[512,1024]{1,0:T(8,128)(2,1)} %get-tuple-element.10, f32[512]{0:T(512)S(1)} %fusion.20), kind=kOutput, calls=%fused_computation.105 | convolution fusion | flops 203816960 | bytes 6426624 | tf_op jit(solution)/shard_map/dot_general | solution.py:48
  86.7 1.6 %fusion.81 = bf16[512,128]{0,1:T(8,128)(2,1)S(1)} fusion(f32[512,1536]{1,0:T(8,128)S(1)} %get-tuple-element.16, f32[512]{0:T(512)S(1)} %get-tuple-element.15, bf16[1024,1024]{1,0:T(8,128)(2,1)S(1)} %bitcast.50, bf16[512,1024]{1,0:T(8,128)(2,1)} %get-tuple-element.10, f32[512]{0:T(512)S(1)} %fusion.18), kind=kOutput, calls=%fused_computation.106 | convolution fusion | flops 203816960 | bytes 6426624 | tf_op jit(solution)/shard_map/dot_general | solution.py:48
  88.9 1.6 %fusion.84 = bf16[512,128]{0,1:T(8,128)(2,1)S(1)} fusion(f32[512,1536]{1,0:T(8,128)S(1)} %get-tuple-element.18, f32[512]{0:T(512)S(1)} %get-tuple-element.17, bf16[1024,1024]{1,0:T(8,128)(2,1)S(1)} %bitcast.51, bf16[512,1024]{1,0:T(8,128)(2,1)} %get-tuple-element.10, f32[512]{0:T(512)S(1)} %fusion.16), kind=kOutput, calls=%fused_computation.107 | convolution fusion | flops 203816960 | bytes 6426624 | tf_op jit(solution)/shard_map/dot_general | solution.py:48
  97.3 1.1 %maximum_bitcast_fusion = bf16[1,2,512,512]{3,2,1,0:T(8,128)(2,1)} fusion(bf16[1,512,512]{2,1,0:T(8,128)(2,1)S(1)} %fusion.50, bf16[1,512,512]{2,1,0:T(8,128)(2,1)S(1)} %fusion.49), kind=kLoop, calls=%fused_computation.114 | loop fusion | flops 524288 | bytes 2097152 | tf_op jit(solution)/shard_map/broadcast_in_dim | solution.py:98
  (38 shorter events, 13.1 us)
Async XLA Ops:
  0.0 3.2 %copy-start = (bf16[512,1536]{1,0:T(8,128)(2,1)S(1)}, bf16[512,1536]{1,0:T(8,128)(2,1)}, u32[]{:S(2)}) copy-start(bf16[512,1536]{1,0:T(8,128)(2,1)} %param.6) | copy-start | bytes 4718596
  5.0 4.8 %copy-start.1 = (bf16[1024,1536]{1,0:T(8,128)(2,1)}, bf16[1024,1536]{1,0:T(8,128)(2,1)S(1)}, u32[]{:S(2)}) copy-start(bf16[1024,1536]{1,0:T(8,128)(2,1)S(1)} %convolution_convert_fusion) | copy-start | bytes 9437188
  5.0 35.2 %copy-start.2 = (s32[64]{0:T(128)S(1)}, s32[64]{0:T(128)}, u32[]{:S(2)}) copy-start(s32[64]{0:T(128)} %param.5) | copy-start | bytes 772
  6.5 29.2 %collective-permute-start.2 = (bf16[512,1024]{1,0:T(8,128)(2,1)}, bf16[512,1024]{1,0:T(8,128)(2,1)}, u32[]{:S(2)}, u32[]{:S(2)}) collective-permute-start(bf16[512,1024]{1,0:T(8,128)(2,1)} %get-tuple-element.10), channel_id=1, source_target_pairs={{1,0},{2,1},{3,2},{4,3},{5,4},{6,5},{7,6},{8,7},{9,8},{10,9},{11,1... | collective-permute-start | bytes 3145736 | tf_op jit(solution)/shard_map/ppermute | solution.py:14
  9.7 32.2 %collective-permute-start = (bf16[512,1024]{1,0:T(8,128)(2,1)S(1)}, bf16[512,1024]{1,0:T(8,128)(2,1)}, u32[]{:S(2)}, u32[]{:S(2)}) collective-permute-start(bf16[512,1024]{1,0:T(8,128)(2,1)S(1)} %get-tuple-element.9), channel_id=1, source_target_pairs={{0,1},{1,2},{2,3},{3,4},{4,5},{5,6},{6,7},{7,8},{8,9},{9,10},{10,1... | collective-permute-start | bytes 3145736 | tf_op jit(solution)/shard_map/ppermute | solution.py:14
  38.3 28.3 %collective-permute-start.3 = (bf16[512,1024]{1,0:T(8,128)(2,1)}, bf16[512,1024]{1,0:T(8,128)(2,1)}, u32[]{:S(2)}, u32[]{:S(2)}) collective-permute-start(bf16[512,1024]{1,0:T(8,128)(2,1)} %broadcast_select_fusion), channel_id=1, source_target_pairs={{1,0},{2,1},{3,2},{4,3},{5,4},{6,5},{7,6},{8,7},{9,8},{10,9},{11,1... | collective-permute-start | bytes 3145736 | tf_op jit(solution)/shard_map/ppermute | solution.py:14
  42.0 34.6 %collective-permute-start.1 = (bf16[512,1024]{1,0:T(8,128)(2,1)}, bf16[512,1024]{1,0:T(8,128)(2,1)S(1)}, u32[]{:S(2)}, u32[]{:S(2)}) collective-permute-start(bf16[512,1024]{1,0:T(8,128)(2,1)} %collective-permute-done), channel_id=1, source_target_pairs={{0,1},{1,2},{2,3},{3,4},{4,5},{5,6},{6,7},{7,8},{8,9},{9,10},{10,1... | collective-permute-start | bytes 3145736 | tf_op jit(solution)/shard_map/ppermute | solution.py:14
  95.3 1.0 %copy-start.3 = (bf16[512,512]{1,0:T(8,128)(2,1)S(1)}, bf16[512,512]{1,0:T(8,128)(2,1)}, u32[]{:S(2)}) copy-start(bf16[512,512]{1,0:T(8,128)(2,1)} %param.7) | copy-start | bytes 1572868
where the time goes:
time: 98.9 us; the launch traced here: 98.3 us
  waiting for transfers between devices  39.7 us (40%)
  matrix products  23.1 us (23%)
  other arithmetic  16.1 us (16%)
  starting transfers between devices  16.1 us (16%)
  local copies, waits for them, and re-layouts  3.15 us (3%)
    ppermute x4, waiting for transfers between devices, from_behind(): return lax.ppermute(block, axis, route)  39.7 us
    ppermute x4, starting transfers between devices, from_behind(): return lax.ppermute(block, axis, route)  16.1 us
    dot_general x8, matrix products, head_scores(): lax.dot_general(query_part, key_part, (((1,), (1,)), ((), ())), preferred...  10.9 us
    dot_general x8, matrix products, attend(): jnp.dot(weights.astype(jnp.bfloat16), values[:, low:high], preferred_elem...  9.53 us
    reduce_sum x8, other arithmetic, attend(): totals = jnp.sum(weights, axis=1, keepdims=True)  4.76 us
    another operation x3, other arithmetic, local(): received = jnp.stack(low_window[::-1] + high_window[::-1], axis=0)  4.18 us
    select_n x1, other arithmetic, local(): high_next = jnp.where(place == count - 1, low_now, high_arrived)  2.63 us
  transfers between devices with their start and end apart: 4, of which 2 were waited for; matrix products, arithmetic and copies ran while one was open for 15% of the time, Pallas kernels for 0%

commit v1 on v0

v1 whole, which is shorter than its diff:
```python
import functools

import jax
import jax.numpy as jnp
from jax import lax
from jax.experimental import pallas as pl
from jax.experimental.pallas import tpu as pltpu
from jax.sharding import PartitionSpec as P

HEADS = 4
HEAD_DIM = 128
WIN = 2
GROUP = 512
WIDTH = 512
CHUNK = 256
CHUNKS = GROUP // CHUNK
FAR = -(2.0**100)
RATE = HEAD_DIM ** (-0.5) * 1.4426950408889634


def normalize(rows):
    wide = rows.astype(jnp.float32)
    factor = lax.rsqrt(jnp.mean(wide * wide, axis=-1, keepdims=True) + 1e-06)
    return (wide * factor).astype(jnp.bfloat16)


def episode_bounds(lengths):
    count = lengths.shape[1]
    row = lax.broadcasted_iota(jnp.int32, (count, count), 0)
    col = lax.broadcasted_iota(jnp.int32, (count, count), 1)
    spread = jnp.broadcast_to(lengths.astype(jnp.float32), (count, count))
    column = jnp.sum(jnp.where(row == col, spread, 0.0), axis=1, keepdims=True)
    row = lax.broadcasted_iota(jnp.int32, (count, 128), 0)
    col = lax.broadcasted_iota(jnp.int32, (count, 128), 1)
    ends = jnp.sum(jnp.where(row <= col, column, 0.0), axis=0, keepdims=True)
    starts = jnp.sum(jnp.where(row < col, column, 0.0), axis=0, keepdims=True)
    return starts, ends


def kernel(
    count,
    frames,
    lengths,
    w_qkv_hbm,
    w_out_hbm,
    out,
    own,
    landed,
    w_qkv,
    w_out,
    queries,
    pairs,
    peaks,
    sums,
    result,
    bounds,
    load_sem,
    store_sem,
    send_sem,
    recv_sem,
):
    place = lax.axis_index("ctx")
    right = lax.rem(place + 1, count)
    left = lax.rem(place + count - 1, count)
    first_place = place == 0
    last_place = place == count - 1

    barrier = pltpu.get_barrier_semaphore()
    for neighbour in (left, right):
        pl.semaphore_signal(
            barrier, inc=1, device_id={"ctx": neighbour}, device_id_type=pl.DeviceIdType.MESH
        )

    loads = [
        pltpu.make_async_copy(frames.at[0], own, load_sem.at[0]),
        pltpu.make_async_copy(w_qkv_hbm, w_qkv, load_sem.at[1]),
        pltpu.make_async_copy(w_out_hbm, w_out, load_sem.at[2]),
    ]
    for load in loads:
        load.start()

    def rows(chunk):
        return pl.ds(chunk * CHUNK, CHUNK)

    def link(half, stage, chunk):
        source = frames.at[0, half, rows(chunk)] if stage == 0 else landed.at[half, 0, rows(chunk)]
        return pltpu.make_async_remote_copy(
            src_ref=source,
            dst_ref=landed.at[half, stage, rows(chunk)],
            send_sem=send_sem.at[half, stage, chunk],
            recv_sem=recv_sem.at[half, stage, chunk],
            device_id={"ctx": right if half == 0 else left},
            device_id_type=pl.DeviceIdType.MESH,
        )

    def inside(stage, chunk):
        source = frames.at[0, 0, rows(chunk)] if stage == 0 else landed.at[0, 0, rows(chunk)]
        return pltpu.make_async_copy(
            source, landed.at[1, stage, rows(chunk)], recv_sem.at[1, stage, chunk]
        )

    def send(stage, chunk):
        link(0, stage, chunk).start()

        @pl.when(jnp.logical_not(first_place))
        def _():
            link(1, stage, chunk).start()

        @pl.when(last_place)
        def _():
            inside(stage, chunk).start()

    def arrive(stage, chunk):
        link(0, stage, chunk).wait_recv()

        @pl.when(jnp.logical_not(last_place))
        def _():
            link(1, stage, chunk).wait_recv()

        @pl.when(last_place)
        def _():
            inside(stage, chunk).wait()

    def sent(stage, chunk):
        link(0, stage, chunk).wait_send()

        @pl.when(jnp.logical_not(first_place))
        def _():
            link(1, stage, chunk).wait_send()

    order = list(range(CHUNKS))[::-1]

    starts, ends = episode_bounds(lengths[...])
    bounds[0:1, :] = starts
    bounds[1:2, :] = ends

    pl.semaphore_wait(barrier, 2)
    for chunk in order:
        send(0, chunk)

    def marks(first, number, inner, outer):
        at = (first + lax.broadcasted_iota(jnp.int32, (number, 128), 0)).astype(jnp.float32)
        within = (at >= bounds[0:1, :]) & (at < bounds[1:2, :])
        return jnp.where(within, inner, outer).astype(jnp.bfloat16)

    def lanes(head):
        return slice(head * 128, head * 128 + 128)

    def wide_lanes(head):
        return slice(head * 256, head * 256 + 256)

    ones = jnp.ones((1, 128), jnp.bfloat16)

    def attend(half, tile, keys, values, key_marks, diagonal, fresh):
        span = pl.ds(tile * CHUNK, CHUNK)
        number = keys.shape[0]
        if diagonal:
            query_at = tile * CHUNK + lax.broadcasted_iota(jnp.int32, (CHUNK, number), 0)
            key_at = lax.broadcasted_iota(jnp.int32, (CHUNK, number), 1)
            behind = key_at <= query_at
        ones_column = jnp.broadcast_to(ones, (number, 128))
        for head in range(HEADS):
            key_part = jnp.concatenate([keys[:, lanes(head)], key_marks], axis=1)
            value_part = jnp.concatenate([values[:, lanes(head)], ones_column], axis=1)
            scores = lax.dot_general(
                queries[half, span, wide_lanes(head)],
                key_part,
                (((1,), (1,)), ((), ())),
                preferred_element_type=jnp.float32,
            )
            if diagonal:
                scores = jnp.where(behind, scores, FAR)
            peak = jnp.max(scores, axis=1, keepdims=True)
            if fresh:
                weights = jnp.exp2((scores - peak) * RATE).astype(jnp.bfloat16)
                sums[half, span, wide_lanes(head)] = jnp.dot(
                    weights, value_part, preferred_element_type=jnp.float32
                )
                peaks[half, span, lanes(head)] = jnp.broadcast_to(peak, (CHUNK, 128))
            else:
                before = peaks[half, span, lanes(head)]
                now = jnp.maximum(before, peak)
                scale = jnp.exp2((before - now) * RATE)
                weights = jnp.exp2((scores - now[:, :1]) * RATE).astype(jnp.bfloat16)
                sums[half, span, wide_lanes(head)] = sums[half, span, wide_lanes(head)] * jnp.concatenate(
                    [scale, scale], axis=1
                ) + jnp.dot(weights, value_part, preferred_element_type=jnp.float32)
                peaks[half, span, lanes(head)] = now

    def block_first(half):
        return GROUP * (place + half * (2 * count - 1 - 2 * place))

    loads[0].wait()
    loads[1].wait()

    def own_half(half, carry):
        base = block_first(half)
        for tile in range(CHUNKS):
            span = slice(tile * CHUNK, tile * CHUNK + CHUNK)
            normed = normalize(own[half, span])
            query_part = jnp.dot(
                normed, w_qkv[:, :WIDTH], preferred_element_type=jnp.float32
            ).astype(jnp.bfloat16)
            query_marks = marks(base + tile * CHUNK, CHUNK, FAR, 0.0)
            for head in range(HEADS):
                queries[half, span, head * 256 : head * 256 + 128] = query_part[:, lanes(head)]
                queries[half, span, head * 256 + 128 : head * 256 + 256] = query_marks
            pairs[span] = jnp.dot(
                normed, w_qkv[:, WIDTH:], preferred_element_type=jnp.float32
            ).astype(jnp.bfloat16)
        for tile in range(CHUNKS):
            number = (tile + 1) * CHUNK
            attend(
                half,
                tile,
                pairs[:number, :WIDTH],
                pairs[:number, WIDTH:],
                marks(base, number, 0.0, 1.0),
                True,
                True,
            )
        return carry

    lax.fori_loop(0, 2, own_half, 0)

    for stage in range(WIN):
        for chunk in order:
            arrive(stage, chunk)
            if stage == 0:
                send(1, chunk)

            def earlier(half, carry):
                normed = normalize(landed[half, stage, rows(chunk)])
                pairs[:CHUNK] = jnp.dot(
                    normed, w_qkv[:, WIDTH:], preferred_element_type=jnp.float32
                ).astype(jnp.bfloat16)
                key_first = block_first(half) - GROUP * (stage + 1) + chunk * CHUNK
                key_marks = marks(key_first, CHUNK, 0.0, 1.0)
                for tile in range(CHUNKS):
                    if stage == 0 or tile <= chunk:
                        attend(
                            half,
                            tile,
                            pairs[:CHUNK, :WIDTH],
                            pairs[:CHUNK, WIDTH:],
                            key_marks,
                            False,
                            False,
                        )
                return carry

            lax.fori_loop(0, 2, earlier, 0)
            if stage == WIN - 1:
                if chunk == order[0]:
                    loads[2].wait()
                span = rows(chunk)
                for half in range(2):
                    mixed = []
                    for head in range(HEADS):
                        total = sums[half, span, wide_lanes(head)]
                        mixed.append((total[:, :128] / total[:, 128:]).astype(jnp.bfloat16))
                    result[half, span] = jnp.dot(
                        jnp.concatenate(mixed, axis=1), w_out[...], preferred_element_type=jnp.float32
                    ).astype(jnp.bfloat16)
                    pltpu.make_async_copy(
                        result.at[half, span], out.at[0, half, span], store_sem.at[half, chunk]
                    ).start()

    for chunk in order:
        for half in range(2):
            span = rows(chunk)
            pltpu.make_async_copy(
                result.at[half, span], out.at[0, half, span], store_sem.at[half, chunk]
            ).wait()
    for stage in range(WIN):
        for chunk in order:
            sent(stage, chunk)


def solution(mesh):
    count = mesh.shape["ctx"]

    def local(frames, episode_lengths, w_qkv, w_out):
        lengths = episode_lengths.reshape(1, -1)
        return pl.pallas_call(
            functools.partial(kernel, count),
            out_shape=jax.ShapeDtypeStruct(frames.shape, jnp.bfloat16),
            in_specs=[
                pl.BlockSpec(memory_space=pltpu.HBM),
                pl.BlockSpec(memory_space=pltpu.VMEM),
                pl.BlockSpec(memory_space=pltpu.HBM),
                pl.BlockSpec(memory_space=pltpu.HBM),
            ],
            out_specs=pl.BlockSpec(memory_space=pl.ANY),
            scratch_shapes=[
                pltpu.VMEM((2, GROUP, WIDTH), jnp.bfloat16),
                pltpu.VMEM((2, WIN, GROUP, WIDTH), jnp.bfloat16),
                pltpu.VMEM((WIDTH, 3 * WIDTH), jnp.bfloat16),
                pltpu.VMEM((WIDTH, WIDTH), jnp.bfloat16),
                pltpu.VMEM((2, GROUP, 2 * WIDTH), jnp.bfloat16),
                pltpu.VMEM((GROUP, 2 * WIDTH), jnp.bfloat16),
                pltpu.VMEM((2, GROUP, WIDTH), jnp.float32),
                pltpu.VMEM((2, GROUP, 2 * WIDTH), jnp.float32),
                pltpu.VMEM((2, GROUP, WIDTH), jnp.bfloat16),
                pltpu.VMEM((8, 128), jnp.float32),
                pltpu.SemaphoreType.DMA((3,)),
                pltpu.SemaphoreType.DMA((2, CHUNKS)),
                pltpu.SemaphoreType.DMA((2, WIN, CHUNKS)),
                pltpu.SemaphoreType.DMA((2, WIN, CHUNKS)),
            ],
            compiler_params=pltpu.CompilerParams(
                collective_id=0, has_side_effects=True, vmem_limit_bytes=48 * 1024 * 1024
            ),
        )(frames, lengths, w_qkv, w_out)

    in_specs = (P(("dp", "ctx"), None, None, None), P("dp"), P(), P())
    out_specs = P(("dp", "ctx"), None, None, None)
    return jax.shard_map(local, mesh=mesh, in_specs=in_specs, out_specs=out_specs, check_vma=False)
```

time: 98.9 us -> 45.8 us (0.46)
  the two profiles are of different devices: /device:TPU:56 before, /device:TPU:448 now
where the time goes in v1:
time: 45.8 us; the launch traced here: 45.5 us
  Pallas kernels  40.2 us (88%)
  local copies, waits for them, and re-layouts  5.3 us (12%)
    pallas_call x1, Pallas kernels, local(): pl.pallas_call(functools.partial(kernel, count), out_shape=jax.ShapeDtype...  40.2 us
    unnamed x9, local copies, waits for them, and re-layouts  5.3 us

profile of v1, /device:TPU:448, one launch (start us, length us, event | category | flops | bytes accessed | tf_op | source)
XLA Modules:
  0.0 45.5 jit_solution(13972281617230381851)
XLA Ops:
  0.0 0.0 copy-start
  0.0 1.4 %copy-done = bf16[512,1536]{1,0:T(8,128)(2,1)S(1)} copy-done((bf16[512,1536]{1,0:T(8,128)(2,1)S(1)}, bf16[512,1536]{1,0:T(8,128)(2,1)}, u32[]{:S(2)}) %copy-start) | copy-done | bytes 1572888
  1.4 0.0 copy-start.1
  1.4 1.2 %copy-done.1 = bf16[1,2,512,512]{3,2,1,0:T(8,128)(2,1)S(1)} copy-done((bf16[1,2,512,512]{3,2,1,0:T(8,128)(2,1)S(1)}, bf16[1,2,512,512]{3,2,1,0:T(8,128)(2,1)}, u32[]{:S(2)}) %copy-start.1) | copy-done | bytes 1048600
  2.6 0.0 copy-start.2
  2.6 1.0 %copy-done.2 = bf16[512,512]{1,0:T(8,128)(2,1)S(1)} copy-done((bf16[512,512]{1,0:T(8,128)(2,1)S(1)}, bf16[512,512]{1,0:T(8,128)(2,1)}, u32[]{:S(2)}) %copy-start.2) | copy-done | bytes 524312
  3.7 0.0 copy-start.3
  3.7 0.7 %copy-done.3 = s32[64]{0:T(128)S(1)} copy-done((s32[64]{0:T(128)S(1)}, s32[64]{0:T(128)}, u32[]{:S(2)}) %copy-start.3) | copy-done | bytes 280
  4.3 40.2 %shard_map.46 = bf16[1,2,512,512]{3,2,1,0:T(8,128)(2,1)S(1)} custom-call(bf16[1,2,512,512]{3,2,1,0:T(8,128)(2,1)S(1)} %copy-done.1, s32[1,64]{1,0:T(1,128)S(1)} %bitcast.1, bf16[512,1536]{1,0:T(8,128)(2,1)S(1)} %copy-done, bf16[512,512]{1,0:T(8,128)(2,1)S(1)} %copy-done.2), custom_call_target="tpu_custom_call" | custom-call | tf_op jit(solution)/shard_map/pallas_call | solution.py:285
  44.5 1.0 %copy.6 = bf16[1,2,512,512]{3,2,1,0:T(8,128)(2,1)} copy(bf16[1,2,512,512]{3,2,1,0:T(8,128)(2,1)S(1)} %shard_map.46) | data formatting | bytes 2097152
Async XLA Ops:
  0.0 1.4 %copy-start = (bf16[512,1536]{1,0:T(8,128)(2,1)S(1)}, bf16[512,1536]{1,0:T(8,128)(2,1)}, u32[]{:S(2)}) copy-start(bf16[512,1536]{1,0:T(8,128)(2,1)} %w_qkv_hbm.1) | copy-start | bytes 4718596
  1.4 1.2 %copy-start.1 = (bf16[1,2,512,512]{3,2,1,0:T(8,128)(2,1)S(1)}, bf16[1,2,512,512]{3,2,1,0:T(8,128)(2,1)}, u32[]{:S(2)}) copy-start(bf16[1,2,512,512]{3,2,1,0:T(8,128)(2,1)} %frames.1) | copy-start | bytes 3145732
  2.6 1.0 %copy-start.2 = (bf16[512,512]{1,0:T(8,128)(2,1)S(1)}, bf16[512,512]{1,0:T(8,128)(2,1)}, u32[]{:S(2)}) copy-start(bf16[512,512]{1,0:T(8,128)(2,1)} %w_out_hbm.1) | copy-start | bytes 1572868
  3.7 0.7 %copy-start.3 = (s32[64]{0:T(128)S(1)}, s32[64]{0:T(128)}, u32[]{:S(2)}) copy-start(s32[64]{0:T(128)} %param.5) | copy-start | bytes 772

commit v2 on v0

v2 whole, which is shorter than its diff:
```python
import functools

import jax
import jax.numpy as jnp
from jax import lax
from jax.experimental import pallas as pl
from jax.experimental.pallas import tpu as pltpu
from jax.sharding import PartitionSpec as P

HEADS = 4
HEAD_DIM = 128
WIN = 2
GROUP = 512
WIDTH = 512
TILE = 256
ROWS = HEAD_DIM + 16
FAR = -(2.0**100)
RATE = HEAD_DIM ** (-0.5) * 1.4426950408889634
NEAR_PIECES = ((256, 256), (0, 256))
FAR_PIECES = ((256, 256), (128, 128), (0, 128))
MESH = pl.DeviceIdType.MESH
NT = (((1,), (1,)), ((), ()))


def normalize(rows):
    wide = rows.astype(jnp.float32)
    factor = lax.rsqrt(jnp.mean(wide * wide, axis=-1, keepdims=True) + 1e-06)
    return (wide * factor).astype(jnp.bfloat16)


def dot(a, b, dims=(((1,), (0,)), ((), ()))):
    return lax.dot_general(a, b, dims, preferred_element_type=jnp.float32)


def episode_bounds(lengths):
    count = lengths.shape[1]
    spread = jnp.broadcast_to(lengths.astype(jnp.float32), (128, count))
    row = lax.broadcasted_iota(jnp.int32, (128, count), 0)
    col = lax.broadcasted_iota(jnp.int32, (128, count), 1)
    column_ends = jnp.sum(jnp.where(col <= row, spread, 0.0), axis=1, keepdims=True)
    column_starts = jnp.sum(jnp.where(col < row, spread, 0.0), axis=1, keepdims=True)
    row = lax.broadcasted_iota(jnp.int32, (128, 128), 0)
    col = lax.broadcasted_iota(jnp.int32, (128, 128), 1)
    ends = jnp.sum(jnp.where(row == col, column_ends, 0.0), axis=0, keepdims=True)
    starts = jnp.sum(jnp.where(row == col, column_starts, 0.0), axis=0, keepdims=True)
    return starts, ends, column_starts, column_ends


def kernel(
    count,
    frames,
    lengths,
    w_qkv_hbm,
    w_out_hbm,
    out,
    own,
    landed,
    w_qkv,
    w_out,
    turned,
    queries,
    query_marks,
    peaks,
    sums,
    result,
    bounds,
    load_sem,
    store_sem,
    send_sem,
    recv_sem,
):
    place = lax.axis_index("ctx")
    right = lax.rem(place + 1, count)
    left = lax.rem(place + count - 1, count)
    first_place = place == 0
    last_place = place == count - 1

    barrier = pltpu.get_barrier_semaphore()
    for neighbour in (left, right):
        pl.semaphore_signal(barrier, inc=1, device_id={"ctx": neighbour}, device_id_type=MESH)

    loads = [
        pltpu.make_async_copy(frames.at[0], own, load_sem.at[0]),
        pltpu.make_async_copy(w_qkv_hbm, w_qkv, load_sem.at[1]),
        pltpu.make_async_copy(w_out_hbm, w_out, load_sem.at[2]),
    ]
    for load in loads:
        load.start()

    def pieces(stage):
        return NEAR_PIECES if stage == 0 else FAR_PIECES

    def rows(stage, piece):
        return pl.ds(*pieces(stage)[piece])

    def link(half, stage, piece):
        span = rows(stage, piece)
        source = frames.at[0, half, span] if stage == 0 else landed.at[half, 0, span]
        return pltpu.make_async_remote_copy(
            src_ref=source,
            dst_ref=landed.at[half, stage, span],
            send_sem=send_sem.at[half, stage, piece],
            recv_sem=recv_sem.at[half, stage, piece],
            device_id={"ctx": right if half == 0 else left},
            device_id_type=MESH,
        )

    def inside(stage, piece):
        span = rows(stage, piece)
        source = frames.at[0, 0, span] if stage == 0 else landed.at[0, 0, span]
        return pltpu.make_async_copy(
            source, landed.at[1, stage, span], recv_sem.at[1, stage, piece]
        )

    def send(stage, piece):
        link(0, stage, piece).start()

        @pl.when(jnp.logical_not(first_place))
        def _():
            link(1, stage, piece).start()

        @pl.when(last_place)
        def _():
            inside(stage, piece).start()

    def arrive(stage, piece):
        link(0, stage, piece).wait_recv()

        @pl.when(jnp.logical_not(last_place))
        def _():
            link(1, stage, piece).wait_recv()

        @pl.when(last_place)
        def _():
            inside(stage, piece).wait()

    def sent(stage, piece):
        link(0, stage, piece).wait_send()

        @pl.when(jnp.logical_not(first_place))
        def _():
            link(1, stage, piece).wait_send()

    def lanes(head):
        return slice(head * 128, head * 128 + 128)

    def block_first(half):
        return GROUP * (place + half * (2 * count - 1 - 2 * place))

    def key_marks(first, number):
        at = (first + lax.broadcasted_iota(jnp.int32, (number, 128), 0)).astype(jnp.float32)
        within = (at >= bounds[0:1, :]) & (at < bounds[1:2, :])
        return jnp.where(within, 0.0, 1.0).astype(jnp.bfloat16)

    def attend(half, first_query, number, keys, values, marks, diagonal, fresh):
        span = slice(first_query, first_query + number)
        keys_here = marks.shape[0]
        ones = jnp.ones((ROWS - HEAD_DIM, keys_here), jnp.bfloat16)
        if diagonal:
            key_at = lax.broadcasted_iota(jnp.int32, (keys_here, number), 0)
            query_at = first_query + lax.broadcasted_iota(jnp.int32, (keys_here, number), 1)
            behind = key_at <= query_at

        def score(head):
            key_part = jnp.concatenate([keys[:, lanes(head)], marks], axis=1)
            query_part = jnp.concatenate(
                [queries[half, lanes(head), span], query_marks[half, :, span]], axis=0
            )
            return dot(key_part, query_part)

        ahead = score(0)
        for head in range(HEADS):
            scores = ahead
            if head + 1 < HEADS:
                ahead = score(head + 1)
            if diagonal:
                scores = jnp.where(behind, scores, FAR)
            peak = jnp.max(scores, axis=0, keepdims=True)
            value_part = jnp.concatenate([values[lanes(head), :], ones], axis=0)
            if fresh:
                weights = jnp.exp2((scores - peak) * RATE).astype(jnp.bfloat16)
                sums[half, head, :, span] = dot(value_part, weights)
                peaks[half, head : head + 1, span] = peak
            else:
                before = peaks[half, head : head + 1, span]
                now = jnp.maximum(before, peak)
                scale = jnp.exp2((before - now) * RATE)
                weights = jnp.exp2((scores - now) * RATE).astype(jnp.bfloat16)
                sums[half, head, :, span] = sums[half, head, :, span] * scale + dot(
                    value_part, weights
                )
                peaks[half, head : head + 1, span] = now

    def project(normed):
        keys = dot(normed, w_qkv[:, WIDTH : 2 * WIDTH]).astype(jnp.bfloat16)
        values = dot(turned[WIDTH:, :], normed, NT).astype(jnp.bfloat16)
        return keys, values

    starts, ends, column_starts, column_ends = episode_bounds(lengths[...])
    bounds[0:1, :] = starts
    bounds[1:2, :] = ends

    pl.semaphore_wait(barrier, 2)
    send(0, 0)
    send(0, 1)

    loads[1].wait()
    turned[:WIDTH, :] = w_qkv[:, :WIDTH].T
    turned[WIDTH:, :] = w_qkv[:, 2 * WIDTH :].T
    loads[0].wait()

    def own_half(half, carry):
        base = block_first(half)
        at = (base + lax.broadcasted_iota(jnp.int32, (128, GROUP), 1)).astype(jnp.float32)
        within = (at >= column_starts) & (at < column_ends)
        query_marks[half] = jnp.where(within, FAR, 0.0).astype(jnp.bfloat16)
        normed = normalize(own[half])
        queries[half] = dot(turned[:WIDTH, :], normed, NT).astype(jnp.bfloat16)
        keys, values = project(normed)
        marks = key_marks(base, GROUP)
        for tile in range(GROUP // TILE):
            number = (tile + 1) * TILE
            attend(half, tile * TILE, TILE, keys[:number], values[:, :number], marks[:number], True, True)
        return carry

    lax.fori_loop(0, 2, own_half, 0)

    def earlier(stage, piece):
        low, number = pieces(stage)[piece]

        def body(half, carry):
            keys, values = project(normalize(landed[half, stage, low : low + number]))
            marks = key_marks(block_first(half) - GROUP * (stage + 1) + low, number)
            limit = GROUP if stage == 0 else low + number
            for first_query in range(0, limit, TILE):
                attend(
                    half, first_query, min(TILE, limit - first_query), keys, values, marks, False, False
                )
            return carry

        lax.fori_loop(0, 2, body, 0)

    def store(half, low, number):
        span = pl.ds(low, number)
        return pltpu.make_async_copy(
            result.at[half, span], out.at[0, half, span], store_sem.at[half, low // 128]
        )

    def finish(low, number):
        span = slice(low, low + number)
        for half in range(2):
            mixed = []
            for head in range(HEADS):
                inverse = 1.0 / sums[half, head, HEAD_DIM : HEAD_DIM + 1, span]
                mixed.append((sums[half, head, :HEAD_DIM, span] * inverse).astype(jnp.bfloat16))
            result[half, span] = dot(jnp.concatenate(mixed, axis=0).T, w_out[...]).astype(jnp.bfloat16)
            store(half, low, number).start()

    arrive(0, 0)
    send(1, 0)
    earlier(0, 0)
    arrive(0, 1)
    send(1, 1)
    send(1, 2)
    earlier(0, 1)
    loads[2].wait()
    for piece, (low, number) in enumerate(FAR_PIECES):
        arrive(1, piece)
        earlier(1, piece)
        finish(low, number)

    for low, number in FAR_PIECES:
        for half in range(2):
            store(half, low, number).wait()
    for stage in range(WIN):
        for piece in range(len(pieces(stage))):
            sent(stage, piece)


def solution(mesh):
    count = mesh.shape["ctx"]

    def local(frames, episode_lengths, w_qkv, w_out):
        lengths = episode_lengths.reshape(1, -1)
        return pl.pallas_call(
            functools.partial(kernel, count),
            out_shape=jax.ShapeDtypeStruct(frames.shape, jnp.bfloat16),
            in_specs=[
                pl.BlockSpec(memory_space=pltpu.HBM),
                pl.BlockSpec(memory_space=pltpu.VMEM),
                pl.BlockSpec(memory_space=pltpu.HBM),
                pl.BlockSpec(memory_space=pltpu.HBM),
            ],
            out_specs=pl.BlockSpec(memory_space=pl.ANY),
            scratch_shapes=[
                pltpu.VMEM((2, GROUP, WIDTH), jnp.bfloat16),
                pltpu.VMEM((2, WIN, GROUP, WIDTH), jnp.bfloat16),
                pltpu.VMEM((WIDTH, 3 * WIDTH), jnp.bfloat16),
                pltpu.VMEM((WIDTH, WIDTH), jnp.bfloat16),
                pltpu.VMEM((2 * WIDTH, WIDTH), jnp.bfloat16),
                pltpu.VMEM((2, WIDTH, GROUP), jnp.bfloat16),
                pltpu.VMEM((2, 128, GROUP), jnp.bfloat16),
                pltpu.VMEM((2, 8, GROUP), jnp.float32),
                pltpu.VMEM((2, HEADS, ROWS, GROUP), jnp.float32),
                pltpu.VMEM((2, GROUP, WIDTH), jnp.bfloat16),
                pltpu.VMEM((8, 128), jnp.float32),
                pltpu.SemaphoreType.DMA((3,)),
                pltpu.SemaphoreType.DMA((2, 4)),
                pltpu.SemaphoreType.DMA((2, WIN, 3)),
                pltpu.SemaphoreType.DMA((2, WIN, 3)),
            ],
            compiler_params=pltpu.CompilerParams(
                collective_id=0, has_side_effects=True, vmem_limit_bytes=62 * 1024 * 1024
            ),
        )(frames, lengths, w_qkv, w_out)

    in_specs = (P(("dp", "ctx"), None, None, None), P("dp"), P(), P())
    out_specs = P(("dp", "ctx"), None, None, None)
    return jax.shard_map(local, mesh=mesh, in_specs=in_specs, out_specs=out_specs, check_vma=False)
```

time: 98.9 us -> 39 us (0.39)
  the two profiles are of different devices: /device:TPU:56 before, /device:TPU:448 now
where the time goes in v2:
time: 39 us; the launch traced here: 38.8 us
  Pallas kernels  36.6 us (94%)
  local copies, waits for them, and re-layouts  2.26 us (6%)
    pallas_call x1, Pallas kernels, local(): pl.pallas_call(functools.partial(kernel, count), out_shape=jax.ShapeDtype...  36.6 us
    unnamed x1, local copies, waits for them, and re-layouts  2.26 us

profile of v2, /device:TPU:448, one launch (start us, length us, event | category | flops | bytes accessed | tf_op | source)
XLA Modules:
  0.0 38.8 jit_solution(1409999418375001659)
XLA Ops:
  0.0 36.6 %shard_map.46 = bf16[1,2,512,512]{3,2,1,0:T(8,128)(2,1)} custom-call(bf16[1,2,512,512]{3,2,1,0:T(8,128)(2,1)} %frames.1, s32[1,64]{1,0:T(1,128)} %bitcast.1, bf16[512,1536]{1,0:T(8,128)(2,1)} %w_qkv_hbm.1, bf16[512,512]{1,0:T(8,128)(2,1)} %w_out_hbm.1), custom_call_target="tpu_custom_call" | custom-call | tf_op jit(solution)/shard_map/pallas_call | solution.py:285
  36.6 2.3 %copy.6 = bf16[1,2,512,512]{3,2,1,0:T(8,128)(2,1)} copy(bf16[1,2,512,512]{3,2,1,0:T(8,128)(2,1)} %shard_map.46) | data formatting | bytes 2097152

commit v3 on v2

--- a/solution.py
+++ b/solution.py
@@ -49,7 +49,7 @@
 def kernel(
     count,
     frames,
-    lengths,
+    lengths_hbm,
     w_qkv_hbm,
     w_out_hbm,
     out,
@@ -64,6 +64,7 @@
     sums,
     result,
     bounds,
+    lengths,
     load_sem,
     store_sem,
     send_sem,
@@ -83,6 +84,7 @@
         pltpu.make_async_copy(frames.at[0], own, load_sem.at[0]),
         pltpu.make_async_copy(w_qkv_hbm, w_qkv, load_sem.at[1]),
         pltpu.make_async_copy(w_out_hbm, w_out, load_sem.at[2]),
+        pltpu.make_async_copy(lengths_hbm, lengths, load_sem.at[3]),
     ]
     for load in loads:
         load.start()
@@ -152,58 +154,62 @@
         within = (at >= bounds[0:1, :]) & (at < bounds[1:2, :])
         return jnp.where(within, 0.0, 1.0).astype(jnp.bfloat16)
 
-    def attend(half, first_query, number, keys, values, marks, diagonal, fresh):
+    def scores_of(half, head, first_query, number, keys, values, marks, diagonal):
+        span = slice(first_query, first_query + number)
+        key_part = jnp.concatenate([keys[:, lanes(head)], marks], axis=1)
+        query_part = jnp.concatenate(
+            [queries[half, lanes(head), span], query_marks[half, :, span]], axis=0
+        )
+        return dot(key_part, query_part)
+
+    def weigh(scores, half, head, first_query, number, keys, values, marks, diagonal):
         span = slice(first_query, first_query + number)
         keys_here = marks.shape[0]
-        ones = jnp.ones((ROWS - HEAD_DIM, keys_here), jnp.bfloat16)
         if diagonal:
             key_at = lax.broadcasted_iota(jnp.int32, (keys_here, number), 0)
             query_at = first_query + lax.broadcasted_iota(jnp.int32, (keys_here, number), 1)
-            behind = key_at <= query_at
-
-        def score(head):
-            key_part = jnp.concatenate([keys[:, lanes(head)], marks], axis=1)
-            query_part = jnp.concatenate(
-                [queries[half, lanes(head), span], query_marks[half, :, span]], axis=0
-            )
-            return dot(key_part, query_part)
-
-        ahead = score(0)
-        for head in range(HEADS):
-            scores = ahead
-            if head + 1 < HEADS:
-                ahead = score(head + 1)
-            if diagonal:
-                scores = jnp.where(behind, scores, FAR)
-            peak = jnp.max(scores, axis=0, keepdims=True)
-            value_part = jnp.concatenate([values[lanes(head), :], ones], axis=0)
-            if fresh:
-                weights = jnp.exp2((scores - peak) * RATE).astype(jnp.bfloat16)
-                sums[half, head, :, span] = dot(value_part, weights)
-                peaks[half, head : head + 1, span] = peak
-            else:
-                before = peaks[half, head : head + 1, span]
-                now = jnp.maximum(before, peak)
-                scale = jnp.exp2((before - now) * RATE)
-                weights = jnp.exp2((scores - now) * RATE).astype(jnp.bfloat16)
-                sums[half, head, :, span] = sums[half, head, :, span] * scale + dot(
-                    value_part, weights
-                )
-                peaks[half, head : head + 1, span] = now
+            scores = jnp.where(key_at <= query_at, scores, FAR)
+        peak = jnp.max(scores, axis=0, keepdims=True)
+        scale = None
+        if not diagonal:
+            before = peaks[half, head : head + 1, span]
+            peak = jnp.maximum(before, peak)
+            scale = jnp.exp2((before - peak) * RATE)
+        peaks[half, head : head + 1, span] = peak
+        return jnp.exp2((scores - peak) * RATE).astype(jnp.bfloat16), scale
+
+    def mix(weights, scale, half, head, first_query, number, keys, values, marks, diagonal):
+        span = slice(first_query, first_query + number)
+        ones = jnp.ones((ROWS - HEAD_DIM, marks.shape[0]), jnp.bfloat16)
+        value_part = jnp.concatenate([values[lanes(head), :], ones], axis=0)
+        total = dot(value_part, weights)
+        if not diagonal:
+            total = sums[half, head, :, span] * scale + total
+        sums[half, head, :, span] = total
+
+    def attend(work):
+        every = [scores_of(*item) for item in work]
+        last = None
+        for scores, item in zip(every, work):
+            weights, scale = weigh(scores, *item)
+            if last is not None:
+                mix(*last)
+            last = (weights, scale, *item)
+        mix(*last)
 
     def project(normed):
         keys = dot(normed, w_qkv[:, WIDTH : 2 * WIDTH]).astype(jnp.bfloat16)
         values = dot(turned[WIDTH:, :], normed, NT).astype(jnp.bfloat16)
         return keys, values
 
+    pl.semaphore_wait(barrier, 2)
+    send(0, 0)
+    send(0, 1)
+
+    loads[3].wait()
     starts, ends, column_starts, column_ends = episode_bounds(lengths[...])
     bounds[0:1, :] = starts
     bounds[1:2, :] = ends
-
-    pl.semaphore_wait(barrier, 2)
-    send(0, 0)
-    send(0, 1)
-
     loads[1].wait()
     turned[:WIDTH, :] = w_qkv[:, :WIDTH].T
     turned[WIDTH:, :] = w_qkv[:, 2 * WIDTH :].T
@@ -218,27 +224,36 @@
         queries[half] = dot(turned[:WIDTH, :], normed, NT).astype(jnp.bfloat16)
         keys, values = project(normed)
         marks = key_marks(base, GROUP)
-        for tile in range(GROUP // TILE):
-            number = (tile + 1) * TILE
-            attend(half, tile * TILE, TILE, keys[:number], values[:, :number], marks[:number], True, True)
+        work = []
+        for first_query in range(0, GROUP, TILE):
+            number = first_query + TILE
+            for head in range(HEADS):
+                work.append(
+                    (half, head, first_query, TILE, keys[:number], values[:, :number], marks[:number], True)
+                )
+        attend(work)
         return carry
 
     lax.fori_loop(0, 2, own_half, 0)
 
-    def earlier(stage, piece):
+    def earlier(stage, piece, together=False):
         low, number = pieces(stage)[piece]
 
-        def body(half, carry):
+        limit = GROUP if stage == 0 else low + number
+
+        def prepare(half):
             keys, values = project(normalize(landed[half, stage, low : low + number]))
             marks = key_marks(block_first(half) - GROUP * (stage + 1) + low, number)
-            limit = GROUP if stage == 0 else low + number
-            for first_query in range(0, limit, TILE):
-                attend(
-                    half, first_query, min(TILE, limit - first_query), keys, values, marks, False, False
-                )
+            return [(half, head, 0, limit, keys, values, marks, False) for head in range(HEADS)]
+
+        def body(half, carry):
+            attend(prepare(half))
             return carry
 
-        lax.fori_loop(0, 2, body, 0)
+        if together:
+            attend(prepare(0) + prepare(1))
+        else:
+            lax.fori_loop(0, 2, body, 0)
 
     def store(half, low, number):
         span = pl.ds(low, number)
@@ -266,7 +281,7 @@
     loads[2].wait()
     for piece, (low, number) in enumerate(FAR_PIECES):
         arrive(1, piece)
-        earlier(1, piece)
+        earlier(1, piece, piece > 0)
         finish(low, number)
 
     for low, number in FAR_PIECES:
@@ -287,7 +302,7 @@
             out_shape=jax.ShapeDtypeStruct(frames.shape, jnp.bfloat16),
             in_specs=[
                 pl.BlockSpec(memory_space=pltpu.HBM),
-                pl.BlockSpec(memory_space=pltpu.VMEM),
+                pl.BlockSpec(memory_space=pltpu.HBM),
                 pl.BlockSpec(memory_space=pltpu.HBM),
                 pl.BlockSpec(memory_space=pltpu.HBM),
             ],
@@ -304,7 +319,8 @@
                 pltpu.VMEM((2, HEADS, ROWS, GROUP), jnp.float32),
                 pltpu.VMEM((2, GROUP, WIDTH), jnp.bfloat16),
                 pltpu.VMEM((8, 128), jnp.float32),
-                pltpu.SemaphoreType.DMA((3,)),
+                pltpu.VMEM(lengths.shape, jnp.int32),
+                pltpu.SemaphoreType.DMA((4,)),
                 pltpu.SemaphoreType.DMA((2, 4)),
                 pltpu.SemaphoreType.DMA((2, WIN, 3)),
                 pltpu.SemaphoreType.DMA((2, WIN, 3)),

time: 39 us -> 35.5 us (0.910)
  Pallas kernels: 36.6 us -> 33 us
    pallas_call x1, Pallas kernels: 36.6 us -> 33 us  [local(): pl.pallas_call(functools.partial(kernel, count), out_shape=jax.ShapeDtype...]
where the time goes in v3:
time: 35.5 us; the launch traced here: 35.3 us
  Pallas kernels  33 us (93%)
  local copies, waits for them, and re-layouts  2.26 us (6%)
    pallas_call x1, Pallas kernels, local(): pl.pallas_call(functools.partial(kernel, count), out_shape=jax.ShapeDtype...  33 us
    unnamed x1, local copies, waits for them, and re-layouts  2.26 us

profile of v3, /device:TPU:448, one launch (start us, length us, event | category | flops | bytes accessed | tf_op | source)
XLA Modules:
  0.0 35.3 jit_solution(2591359942050722029)
XLA Ops:
  0.0 33.0 %shard_map.46 = bf16[1,2,512,512]{3,2,1,0:T(8,128)(2,1)} custom-call(bf16[1,2,512,512]{3,2,1,0:T(8,128)(2,1)} %frames.1, s32[1,64]{1,0:T(1,128)} %bitcast.1, bf16[512,1536]{1,0:T(8,128)(2,1)} %w_qkv_hbm.1, bf16[512,512]{1,0:T(8,128)(2,1)} %w_out_hbm.1), custom_call_target="tpu_custom_call" | custom-call | tf_op jit(solution)/shard_map/pallas_call | solution.py:300
  33.0 2.3 %copy.6 = bf16[1,2,512,512]{3,2,1,0:T(8,128)(2,1)} copy(bf16[1,2,512,512]{3,2,1,0:T(8,128)(2,1)} %shard_map.46) | data formatting | bytes 2097152

commit v4 on v3

--- a/solution.py
+++ b/solution.py
@@ -62,11 +62,9 @@
     query_marks,
     peaks,
     sums,
-    result,
     bounds,
     lengths,
     load_sem,
-    store_sem,
     send_sem,
     recv_sem,
 ):
@@ -241,35 +239,38 @@
 
         limit = GROUP if stage == 0 else low + number
 
-        def prepare(half):
-            keys, values = project(normalize(landed[half, stage, low : low + number]))
+        def prepare(half, keys, values):
             marks = key_marks(block_first(half) - GROUP * (stage + 1) + low, number)
             return [(half, head, 0, limit, keys, values, marks, False) for head in range(HEADS)]
 
-        def body(half, carry):
-            attend(prepare(half))
-            return carry
-
+        span = slice(low, low + number)
         if together:
-            attend(prepare(0) + prepare(1))
+            both = jnp.concatenate([landed[0, stage, span], landed[1, stage, span]], axis=0)
+            keys, values = project(normalize(both))
+            attend(
+                prepare(0, keys[:number], values[:, :number])
+                + prepare(1, keys[number:], values[:, number:])
+            )
         else:
+
+            def body(half, carry):
+                attend(prepare(half, *project(normalize(landed[half, stage, span]))))
+                return carry
+
             lax.fori_loop(0, 2, body, 0)
-
-    def store(half, low, number):
-        span = pl.ds(low, number)
-        return pltpu.make_async_copy(
-            result.at[half, span], out.at[0, half, span], store_sem.at[half, low // 128]
-        )
 
     def finish(low, number):
         span = slice(low, low + number)
+        mixed = []
         for half in range(2):
-            mixed = []
+            parts = []
             for head in range(HEADS):
                 inverse = 1.0 / sums[half, head, HEAD_DIM : HEAD_DIM + 1, span]
-                mixed.append((sums[half, head, :HEAD_DIM, span] * inverse).astype(jnp.bfloat16))
-            result[half, span] = dot(jnp.concatenate(mixed, axis=0).T, w_out[...]).astype(jnp.bfloat16)
-            store(half, low, number).start()
+                parts.append((sums[half, head, :HEAD_DIM, span] * inverse).astype(jnp.bfloat16))
+            mixed.append(jnp.concatenate(parts, axis=0).T)
+        result = dot(jnp.concatenate(mixed, axis=0), w_out[...]).astype(jnp.bfloat16)
+        out[0, 0, span] = result[:number]
+        out[0, 1, span] = result[number:]
 
     arrive(0, 0)
     send(1, 0)
@@ -284,9 +285,6 @@
         earlier(1, piece, piece > 0)
         finish(low, number)
 
-    for low, number in FAR_PIECES:
-        for half in range(2):
-            store(half, low, number).wait()
     for stage in range(WIN):
         for piece in range(len(pieces(stage))):
             sent(stage, piece)
@@ -299,14 +297,14 @@
         lengths = episode_lengths.reshape(1, -1)
         return pl.pallas_call(
             functools.partial(kernel, count),
-            out_shape=jax.ShapeDtypeStruct(frames.shape, jnp.bfloat16),
+            out_shape=pltpu.VMEM(frames.shape, jnp.bfloat16),
             in_specs=[
                 pl.BlockSpec(memory_space=pltpu.HBM),
                 pl.BlockSpec(memory_space=pltpu.HBM),
                 pl.BlockSpec(memory_space=pltpu.HBM),
                 pl.BlockSpec(memory_space=pltpu.HBM),
             ],
-            out_specs=pl.BlockSpec(memory_space=pl.ANY),
+            out_specs=pl.BlockSpec(memory_space=pltpu.VMEM),
             scratch_shapes=[
                 pltpu.VMEM((2, GROUP, WIDTH), jnp.bfloat16),
                 pltpu.VMEM((2, WIN, GROUP, WIDTH), jnp.bfloat16),
@@ -317,16 +315,14 @@
                 pltpu.VMEM((2, 128, GROUP), jnp.bfloat16),
                 pltpu.VMEM((2, 8, GROUP), jnp.float32),
                 pltpu.VMEM((2, HEADS, ROWS, GROUP), jnp.float32),
-                pltpu.VMEM((2, GROUP, WIDTH), jnp.bfloat16),
                 pltpu.VMEM((8, 128), jnp.float32),
                 pltpu.VMEM(lengths.shape, jnp.int32),
                 pltpu.SemaphoreType.DMA((4,)),
-                pltpu.SemaphoreType.DMA((2, 4)),
                 pltpu.SemaphoreType.DMA((2, WIN, 3)),
                 pltpu.SemaphoreType.DMA((2, WIN, 3)),
             ],
             compiler_params=pltpu.CompilerParams(
-                collective_id=0, has_side_effects=True, vmem_limit_bytes=62 * 1024 * 1024
+                collective_id=0, has_side_effects=True, vmem_limit_bytes=58 * 1024 * 1024
             ),
         )(frames, lengths, w_qkv, w_out)
 

time: 35.5 us -> 33.3 us (0.938)
  local copies, waits for them, and re-layouts: 2.26 us -> 0.97 us
  Pallas kernels: 33 us -> 32.2 us
    unnamed x1, local copies, waits for them, and re-layouts: 2.26 us -> 0.97 us
    pallas_call x1, Pallas kernels: 33 us -> 32.2 us  [local(): pl.pallas_call(functools.partial(kernel, count), out_shape=pltpu.VMEM(fra...]
where the time goes in v4:
time: 33.3 us; the launch traced here: 33.2 us
  Pallas kernels  32.2 us (97%)
  local copies, waits for them, and re-layouts  0.97 us (3%)
    pallas_call x1, Pallas kernels, local(): pl.pallas_call(functools.partial(kernel, count), out_shape=pltpu.VMEM(fra...  32.2 us
    unnamed x1, local copies, waits for them, and re-layouts  0.97 us

profile of v4, /device:TPU:448, one launch (start us, length us, event | category | flops | bytes accessed | tf_op | source)
XLA Modules:
  0.0 33.2 jit_solution(2562062997279363023)
XLA Ops:
  0.0 32.2 %shard_map.46 = bf16[1,2,512,512]{3,2,1,0:T(8,128)(2,1)S(1)} custom-call(bf16[1,2,512,512]{3,2,1,0:T(8,128)(2,1)} %frames.1, s32[1,64]{1,0:T(1,128)} %bitcast.1, bf16[512,1536]{1,0:T(8,128)(2,1)} %w_qkv_hbm.1, bf16[512,512]{1,0:T(8,128)(2,1)} %w_out_hbm.1), custom_call_target="tpu_custom_call" | custom-call | tf_op jit(solution)/shard_map/pallas_call | solution.py:298
  32.2 1.0 %copy.6 = bf16[1,2,512,512]{3,2,1,0:T(8,128)(2,1)} copy(bf16[1,2,512,512]{3,2,1,0:T(8,128)(2,1)S(1)} %shard_map.46) | data formatting | bytes 2097152

commit v5 on v4

--- a/solution.py
+++ b/solution.py
@@ -53,16 +53,19 @@
     w_qkv_hbm,
     w_out_hbm,
     out,
+    waiting,
+    w_out,
     own,
     landed,
     w_qkv,
-    w_out,
     turned,
     queries,
     query_marks,
     peaks,
     sums,
     bounds,
+    folded,
+    barred,
     lengths,
     load_sem,
     send_sem,
@@ -259,6 +262,48 @@
 
             lax.fori_loop(0, 2, body, 0)
 
+    def fold(half, carry):
+        marks = key_marks(block_first(half) - GROUP * WIN, 128)
+        barred[half] = dot(marks, query_marks[half, :, :128])
+        for head in range(HEADS):
+            key_weights = w_qkv[:, WIDTH + head * 128 : WIDTH + head * 128 + 128]
+            folded[half, :, lanes(head)] = dot(key_weights, queries[half, lanes(head), :128]).astype(
+                jnp.bfloat16
+            )
+        return carry
+
+    def last():
+        both = jnp.concatenate([landed[0, 1, :128], landed[1, 1, :128]], axis=0)
+        normed = normalize(both)
+        every = []
+        for half in range(2):
+            scores = dot(normed[half * 128 : half * 128 + 128], folded[half])
+            every += [scores[:, lanes(head)] + barred[half] for head in range(HEADS)]
+        values = dot(turned[WIDTH:, :], normed, NT).astype(jnp.bfloat16)
+        marks = jnp.zeros((128, 128), jnp.bfloat16)
+        ones = jnp.ones((ROWS - HEAD_DIM, 128), jnp.bfloat16)
+        for half in range(2):
+            for head in range(0, HEADS, 2):
+                weights, scales, parts = [], [], []
+                for one in (head, head + 1):
+                    found = weigh(every[half * HEADS + one], half, one, 0, 128, None, None, marks, False)
+                    weights.append(found[0])
+                    scales.append(found[1])
+                    part = values[lanes(one), half * 128 : half * 128 + 128]
+                    parts.append(jnp.concatenate([part, ones], axis=0))
+                blocks = jnp.concatenate(
+                    [
+                        jnp.concatenate([weights[0], marks], axis=1),
+                        jnp.concatenate([marks, weights[1]], axis=1),
+                    ],
+                    axis=0,
+                )
+                total = dot(jnp.concatenate(parts, axis=1), blocks)
+                for one in range(2):
+                    sums[half, head + one, :, :128] = (
+                        sums[half, head + one, :, :128] * scales[one] + total[:, lanes(one)]
+                    )
+
     def finish(low, number):
         span = slice(low, low + number)
         mixed = []
@@ -268,9 +313,13 @@
                 inverse = 1.0 / sums[half, head, HEAD_DIM : HEAD_DIM + 1, span]
                 parts.append((sums[half, head, :HEAD_DIM, span] * inverse).astype(jnp.bfloat16))
             mixed.append(jnp.concatenate(parts, axis=0).T)
+        if low == 0:
+            waiting[...] = jnp.concatenate(mixed, axis=0)
+            return
         result = dot(jnp.concatenate(mixed, axis=0), w_out[...]).astype(jnp.bfloat16)
-        out[0, 0, span] = result[:number]
-        out[0, 1, span] = result[number:]
+        done = slice(low - 128, low - 128 + number)
+        out[0, done] = result[:number]
+        out[1, done] = result[number:]
 
     arrive(0, 0)
     send(1, 0)
@@ -279,10 +328,14 @@
     send(1, 1)
     send(1, 2)
     earlier(0, 1)
+    lax.fori_loop(0, 2, fold, 0)
     loads[2].wait()
     for piece, (low, number) in enumerate(FAR_PIECES):
         arrive(1, piece)
-        earlier(1, piece, piece > 0)
+        if low > 0:
+            earlier(1, piece, piece > 0)
+        else:
+            last()
         finish(low, number)
 
     for stage in range(WIN):
@@ -290,41 +343,77 @@
             sent(stage, piece)
 
 
+def unload(done, waiting, w_out, out, result, sem):
+    copies = [
+        pltpu.make_async_copy(done.at[half], out.at[0, half, pl.ds(128, GROUP - 128)], sem.at[half])
+        for half in range(2)
+    ]
+    for copy in copies:
+        copy.start()
+    result[...] = dot(waiting[...], w_out[...]).astype(jnp.bfloat16)
+    lasts = [
+        pltpu.make_async_copy(
+            result.at[pl.ds(half * 128, 128)], out.at[0, half, pl.ds(0, 128)], sem.at[2 + half]
+        )
+        for half in range(2)
+    ]
+    for copy in lasts:
+        copy.start()
+    for copy in copies + lasts:
+        copy.wait()
+
+
 def solution(mesh):
     count = mesh.shape["ctx"]
 
     def local(frames, episode_lengths, w_qkv, w_out):
         lengths = episode_lengths.reshape(1, -1)
-        return pl.pallas_call(
+        parts = pl.pallas_call(
             functools.partial(kernel, count),
-            out_shape=pltpu.VMEM(frames.shape, jnp.bfloat16),
+            out_shape=(
+                pltpu.VMEM((2, GROUP - 128, WIDTH), jnp.bfloat16),
+                pltpu.VMEM((256, WIDTH), jnp.bfloat16),
+                pltpu.VMEM((WIDTH, WIDTH), jnp.bfloat16),
+            ),
             in_specs=[
                 pl.BlockSpec(memory_space=pltpu.HBM),
                 pl.BlockSpec(memory_space=pltpu.HBM),
                 pl.BlockSpec(memory_space=pltpu.HBM),
                 pl.BlockSpec(memory_space=pltpu.HBM),
             ],
-            out_specs=pl.BlockSpec(memory_space=pltpu.VMEM),
+            out_specs=[pl.BlockSpec(memory_space=pltpu.VMEM)] * 3,
             scratch_shapes=[
                 pltpu.VMEM((2, GROUP, WIDTH), jnp.bfloat16),
                 pltpu.VMEM((2, WIN, GROUP, WIDTH), jnp.bfloat16),
                 pltpu.VMEM((WIDTH, 3 * WIDTH), jnp.bfloat16),
-                pltpu.VMEM((WIDTH, WIDTH), jnp.bfloat16),
                 pltpu.VMEM((2 * WIDTH, WIDTH), jnp.bfloat16),
                 pltpu.VMEM((2, WIDTH, GROUP), jnp.bfloat16),
                 pltpu.VMEM((2, 128, GROUP), jnp.bfloat16),
                 pltpu.VMEM((2, 8, GROUP), jnp.float32),
                 pltpu.VMEM((2, HEADS, ROWS, GROUP), jnp.float32),
                 pltpu.VMEM((8, 128), jnp.float32),
+                pltpu.VMEM((2, WIDTH, WIDTH), jnp.bfloat16),
+                pltpu.VMEM((2, 128, 128), jnp.float32),
                 pltpu.VMEM(lengths.shape, jnp.int32),
                 pltpu.SemaphoreType.DMA((4,)),
                 pltpu.SemaphoreType.DMA((2, WIN, 3)),
                 pltpu.SemaphoreType.DMA((2, WIN, 3)),
             ],
             compiler_params=pltpu.CompilerParams(
-                collective_id=0, has_side_effects=True, vmem_limit_bytes=58 * 1024 * 1024
+                collective_id=0, has_side_effects=True, vmem_limit_bytes=56 * 1024 * 1024
             ),
         )(frames, lengths, w_qkv, w_out)
+        return pl.pallas_call(
+            unload,
+            out_shape=jax.ShapeDtypeStruct(frames.shape, jnp.bfloat16),
+            in_specs=[pl.BlockSpec(memory_space=pltpu.VMEM)] * 3,
+            out_specs=pl.BlockSpec(memory_space=pltpu.HBM),
+            scratch_shapes=[
+                pltpu.VMEM((256, WIDTH), jnp.bfloat16),
+                pltpu.SemaphoreType.DMA((4,)),
+            ],
+            compiler_params=pltpu.CompilerParams(vmem_limit_bytes=4 * 1024 * 1024),
+        )(*parts)
 
     in_specs = (P(("dp", "ctx"), None, None, None), P("dp"), P(), P())
     out_specs = P(("dp", "ctx"), None, None, None)

time: 33.3 us -> 33.2 us (level)
  local copies, waits for them, and re-layouts: 0.97 us -> 0 us
  Pallas kernels: 32.2 us -> 33.1 us
    unnamed x1 -> x0, local copies, waits for them, and re-layouts: 0.97 us -> none
    pallas_call x1 -> x2, Pallas kernels: 32.2 us -> 33.1 us  [the longest x1 32.1 us: local(): pl.pallas_call(functools.partial(kernel, count), out_shape=(pltpu.VMEM((2...]
where the time goes in v5:
time: 33.2 us; the launch traced here: 33.1 us
  Pallas kernels  33.1 us (100%)
    pallas_call x1, Pallas kernels, local(): pl.pallas_call(functools.partial(kernel, count), out_shape=(pltpu.VMEM((2...  32.1 us
    pallas_call x1, Pallas kernels, local(): pl.pallas_call(unload, out_shape=jax.ShapeDtypeStruct(frames.shape, jnp.b...  1.04 us

profile of v5, /device:TPU:448, one launch (start us, length us, event | category | flops | bytes accessed | tf_op | source)
XLA Modules:
  0.0 33.1 jit_solution(8329595815704945815)
XLA Ops:
  0.0 32.1 %shard_map.46 = (bf16[2,384,512]{2,1,0:T(8,128)(2,1)S(1)}, bf16[256,512]{1,0:T(8,128)(2,1)S(1)}, bf16[512,512]{1,0:T(8,128)(2,1)S(1)}) custom-call(bf16[1,2,512,512]{3,2,1,0:T(8,128)(2,1)} %frames.1, s32[1,64]{1,0:T(1,128)} %bitcast.1, bf16[512,1536]{1,0:T(8,128)(2,1)} %w_qkv_hbm.1, bf16[512,512]{1,0:T(8,128)(2,1)} %w_out_hbm.1), custom_call_target="tpu_custom_call" | custom-call | tf_op jit(solution)/shard_map/pallas_call | solution.py:371
  32.1 1.0 %shard_map.47 = bf16[1,2,512,512]{3,2,1,0:T(8,128)(2,1)} custom-call(bf16[2,384,512]{2,1,0:T(8,128)(2,1)S(1)} %get-tuple-element.8.done, bf16[256,512]{1,0:T(8,128)(2,1)S(1)} %get-tuple-element.9.waiting, bf16[512,512]{1,0:T(8,128)(2,1)S(1)} %get-tuple-element.10.w_out), custom_call_target="tpu_custom_call" | custom-call | tf_op jit(solution)/shard_map/pallas_call | solution.py:406

commit v6 on v5

--- a/solution.py
+++ b/solution.py
@@ -300,9 +300,10 @@
                 )
                 total = dot(jnp.concatenate(parts, axis=1), blocks)
                 for one in range(2):
-                    sums[half, head + one, :, :128] = (
-                        sums[half, head + one, :, :128] * scales[one] + total[:, lanes(one)]
-                    )
+                    whole = sums[half, head + one, :, :128] * scales[one] + total[:, lanes(one)]
+                    inverse = 1.0 / whole[HEAD_DIM : HEAD_DIM + 1]
+                    done = (whole[:HEAD_DIM] * inverse).astype(jnp.bfloat16)
+                    waiting[half * 128 : half * 128 + 128, lanes(head + one)] = done.T
 
     def finish(low, number):
         span = slice(low, low + number)
@@ -313,9 +314,6 @@
                 inverse = 1.0 / sums[half, head, HEAD_DIM : HEAD_DIM + 1, span]
                 parts.append((sums[half, head, :HEAD_DIM, span] * inverse).astype(jnp.bfloat16))
             mixed.append(jnp.concatenate(parts, axis=0).T)
-        if low == 0:
-            waiting[...] = jnp.concatenate(mixed, axis=0)
-            return
         result = dot(jnp.concatenate(mixed, axis=0), w_out[...]).astype(jnp.bfloat16)
         done = slice(low - 128, low - 128 + number)
         out[0, done] = result[:number]
@@ -336,7 +334,8 @@
             earlier(1, piece, piece > 0)
         else:
             last()
-        finish(low, number)
+        if low > 0:
+            finish(low, number)
 
     for stage in range(WIN):
         for piece in range(len(pieces(stage))):

time: 33.2 us -> 33.2 us (level)
  no operation moved by 1% of the time
where the time goes in v6:
time: 33.2 us; the launch traced here: 33.1 us
  Pallas kernels  33.1 us (100%)
    pallas_call x1, Pallas kernels, local(): pl.pallas_call(functools.partial(kernel, count), out_shape=(pltpu.VMEM((2...  32 us
    pallas_call x1, Pallas kernels, local(): pl.pallas_call(unload, out_shape=jax.ShapeDtypeStruct(frames.shape, jnp.b...  1.04 us

profile of v6, /device:TPU:448, one launch (start us, length us, event | category | flops | bytes accessed | tf_op | source)
XLA Modules:
  0.0 33.1 jit_solution(5206222774902903565)
XLA Ops:
  0.0 32.0 %shard_map.46 = (bf16[2,384,512]{2,1,0:T(8,128)(2,1)S(1)}, bf16[256,512]{1,0:T(8,128)(2,1)S(1)}, bf16[512,512]{1,0:T(8,128)(2,1)S(1)}) custom-call(bf16[1,2,512,512]{3,2,1,0:T(8,128)(2,1)} %frames.1, s32[1,64]{1,0:T(1,128)} %bitcast.1, bf16[512,1536]{1,0:T(8,128)(2,1)} %w_qkv_hbm.1, bf16[512,512]{1,0:T(8,128)(2,1)} %w_out_hbm.1), custom_call_target="tpu_custom_call" | custom-call | tf_op jit(solution)/shard_map/pallas_call | solution.py:370
  32.1 1.0 %shard_map.47 = bf16[1,2,512,512]{3,2,1,0:T(8,128)(2,1)} custom-call(bf16[2,384,512]{2,1,0:T(8,128)(2,1)S(1)} %get-tuple-element.8.done, bf16[256,512]{1,0:T(8,128)(2,1)S(1)} %get-tuple-element.9.waiting, bf16[512,512]{1,0:T(8,128)(2,1)S(1)} %get-tuple-element.10.w_out), custom_call_target="tpu_custom_call" | custom-call | tf_op jit(solution)/shard_map/pallas_call | solution.py:405
